TPU v7x, 128 devices: a whole 4x4x4 slice. The times are simulated.
128 devices in a mesh: ctx: 16 (over y_lo, z, core), tp: 8 (over y_hi, x).
Axes of the slice: x: 4, y: 4 (y_hi: 2, y_lo: 2; y = y_hi * 2 + y_lo), z: 4, core: 2. Of those that a mesh axis runs over, the one named last changes fastest.
Arguments:
- tokens: bfloat16 [4096, 16384], P('tp', 'ctx'), may hold values from -6 to 6
- in_weight: bfloat16 [3, 4096, 4096], P(None, 'ctx', 'tp'), may hold values from -0.09375 to 0.09375
- short_taps: float32 [3, 4096, 3], P(None, 'tp'), may hold values from -3 to 3
- long_filter: float32 [4096, 16384], P('tp', 'ctx'), may hold values from -2 to 2
- skip_gain: float32 [4096], P('tp'), may hold values from -4 to 4
- out_weight: bfloat16 [4096, 4096], P('tp', 'ctx'), may hold values from -0.125 to 0.125
Outputs:
- layer_out: bfloat16 [4096, 16384], P('tp', 'ctx')
All inputs are finite; a program needn't handle non-finite values.
Results may differ from a plain program's by a relative error of at most 0.02.
Values may be sent and summed in bfloat16 or wider, within the bound.
A program may use at most 128 MiB of HBM per device.

v0:
```python
import math
import jax
import jax.numpy as jnp
from jax import lax
from jax.sharding import PartitionSpec as P

HIGHEST = lax.Precision.HIGHEST


def passed_along(shard, axis, by):
    count = lax.axis_size(axis)
    pairs = [(i, i + by) for i in range(count) if 0 <= i + by < count]
    return lax.ppermute(shard, axis, pairs)


def factor_length(full_len):
    inner_len = 1
    while inner_len * inner_len * 4 <= full_len and full_len % (inner_len * 2) == 0:
        inner_len = inner_len * 2
    return (inner_len, full_len // inner_len)


def phase_table(rows_count, cols_count, period):
    row_ids = jnp.arange(rows_count, dtype=jnp.int32)[:, None]
    col_ids = jnp.arange(cols_count, dtype=jnp.int32)[None, :]
    angles = (row_ids * col_ids % period).astype(jnp.float32) * (2.0 * math.pi / period)
    return (jnp.cos(angles), jnp.sin(angles))


def make_tables(full_len):
    inner_len, outer_len = factor_length(full_len)
    cos_inner, sin_inner = phase_table(inner_len, inner_len, inner_len)
    cos_outer, sin_outer = phase_table(outer_len // 2, outer_len, outer_len)
    cos_twist, sin_twist = phase_table(outer_len, inner_len, full_len)
    return (cos_inner, sin_inner, cos_outer, sin_outer, cos_twist, sin_twist)


def spectrum(signal, tables):
    cos_inner, sin_inner, cos_outer, sin_outer, cos_twist, sin_twist = tables
    channels = signal.shape[0]
    grid_view = signal.reshape(channels, cos_outer.shape[0], cos_inner.shape[0])
    part_re = jnp.einsum("cmn,mk->ckn", grid_view, cos_outer, precision=HIGHEST)
    part_im = -jnp.einsum("cmn,mk->ckn", grid_view, sin_outer, precision=HIGHEST)
    twist_re = part_re * cos_twist + part_im * sin_twist
    twist_im = part_im * cos_twist - part_re * sin_twist
    freq_re = jnp.einsum("ckn,nj->ckj", twist_re, cos_inner, precision=HIGHEST) + jnp.einsum(
        "ckn,nj->ckj", twist_im, sin_inner, precision=HIGHEST
    )
    freq_im = jnp.einsum("ckn,nj->ckj", twist_im, cos_inner, precision=HIGHEST) - jnp.einsum(
        "ckn,nj->ckj", twist_re, sin_inner, precision=HIGHEST
    )
    return (freq_re, freq_im)


def spectrum_back(freq_re, freq_im, tables):
    cos_inner, sin_inner, cos_outer, sin_outer, cos_twist, sin_twist = tables
    mix_re = jnp.einsum("ckj,jn->ckn", freq_re, cos_inner, precision=HIGHEST) - jnp.einsum(
        "ckj,jn->ckn", freq_im, sin_inner, precision=HIGHEST
    )
    mix_im = jnp.einsum("ckj,jn->ckn", freq_im, cos_inner, precision=HIGHEST) + jnp.einsum(
        "ckj,jn->ckn", freq_re, sin_inner, precision=HIGHEST
    )
    turn_re = mix_re * cos_twist - mix_im * sin_twist
    turn_im = mix_im * cos_twist + mix_re * sin_twist
    channels = freq_re.shape[0]
    length = cos_outer.shape[0] * cos_inner.shape[0]
    norm_factor = 1.0 / (cos_outer.shape[1] * cos_inner.shape[0])
    real_out = jnp.einsum("ckn,mk->cmn", turn_re, cos_outer, precision=HIGHEST) - jnp.einsum(
        "ckn,mk->cmn", turn_im, sin_outer, precision=HIGHEST
    )
    real_out = real_out.reshape(channels, length) * norm_factor
    return real_out


def per_device(tokens, in_weight, short_taps, long_filter, skip_gain, out_weight):
    steps_dev = tokens.shape[1]
    filter_groups = lax.all_to_all(
        long_filter.astype(jnp.bfloat16), "ctx", split_axis=0, concat_axis=1, tiled=True
    ).astype(long_filter.dtype)
    features_all = lax.all_gather(tokens, "tp", axis=0, tiled=True)
    sources = (features_all,)
    shard_rows = lax.all_gather(in_weight, "ctx", axis=1, tiled=True)
    results = tuple(
        (
            jnp.einsum("sic,it->sct", shard_rows, source, preferred_element_type=jnp.float32)
            for source in sources
        )
    )
    projected = results[0]
    before = passed_along(projected[:, :, steps_dev - 2 :], "ctx", 1)
    prev_one = jnp.concatenate([before[:, :, 1:], projected[:, :, :-1]], axis=2)
    prev_two = jnp.concatenate([before, projected[:, :, :-2]], axis=2)
    mixed_short = (
        short_taps[:, :, 0:1] * projected
        + short_taps[:, :, 1:2] * prev_one
        + short_taps[:, :, 2:3] * prev_two
    )
    gated_rows = (mixed_short[1] * mixed_short[2]).astype(jnp.bfloat16)
    signal = lax.all_to_all(gated_rows, "ctx", split_axis=0, concat_axis=1, tiled=True)
    tables = make_tables(2 * signal.shape[1])
    sig_re, sig_im = spectrum(signal.astype(jnp.float32), tables)
    fil_re, fil_im = spectrum(filter_groups, tables)
    prod_re = sig_re * fil_re - sig_im * fil_im
    prod_im = sig_re * fil_im + sig_im * fil_re
    long_rows = spectrum_back(prod_re, prod_im, tables)
    long_rows = long_rows.astype(jnp.bfloat16)
    returned = lax.all_to_all(long_rows, "ctx", split_axis=1, concat_axis=0, tiled=True)
    hidden = (
        (returned.astype(jnp.float32) + skip_gain[:, None] * gated_rows.astype(jnp.float32))
        * mixed_short[0]
    ).astype(jnp.bfloat16)
    whole_out = lax.all_gather(out_weight, "ctx", axis=1, tiled=True)
    return lax.psum_scatter(
        jnp.einsum("cd,ct->dt", whole_out, hidden, preferred_element_type=jnp.float32).astype(
            jnp.bfloat16
        ),
        "tp",
        scatter_dimension=0,
        tiled=True,
    )


def solution(mesh):
    placed = (
        P("tp", "ctx"),
        P(None, "ctx", "tp"),
        P(None, "tp", None),
        P("tp", "ctx"),
        P("tp"),
        P("tp", "ctx"),
    )
    return jax.shard_map(
        per_device, mesh=mesh, in_specs=placed, out_specs=P("tp", "ctx"), check_vma=False
    )
```

profile of v0, /device:TPU:1, one launch (start us, length us, event | category | flops | bytes accessed | tf_op | source)
XLA Modules:
  0.0 480.2 jit_solution(12676117775673328608)
XLA Ops:
  10.8 7.8 %all-to-all-start.1 = ((bf16[16,32,1024]{2,1,0:T(8,128)(2,1)}), bf16[16,32,1024]{2,1,0:T(8,128)(2,1)S(1)}, u32[]{:S(2)}, u32[]{:S(2)}) async-start(bf16[16,32,1024]{2,1,0:T(8,128)(2,1)} %bitcast.11), calls=%async_computation.1 | async-start | bytes 2097152 | tf_op jit(solution)/shard_map/all_to_all | solution.py:77
  20.0 19.7 %all-to-all-done.1 = bf16[16,32,1024]{2,1,0:T(8,128)(2,1)S(1)} async-done(((bf16[16,32,1024]{2,1,0:T(8,128)(2,1)}), bf16[16,32,1024]{2,1,0:T(8,128)(2,1)S(1)}, u32[]{:S(2)}, u32[]{:S(2)}) %all-to-all-start.1) | async-done | bytes 1048608 | tf_op jit(solution)/shard_map/all_to_all | solution.py:77
  47.4 5.6 %fusion.6 = f32[32,256,128]{2,1,0:T(8,128)} fusion(f32[256,32,128]{2,0,1:T(8,128)S(1)} %fusion.64, f32[256,32,128]{2,0,1:T(8,128)S(1)} %fusion.60, f32[256,128]{1,0:T(8,128)S(1)} %get-tuple-element.12, f32[256,128]{1,0:T(8,128)S(1)} %get-tuple-element.13), kind=kOutput, calls=%fused_computation.9 | convolution fusion | flops 1615036416 | bytes 12845056 | tf_op jit(solution)/shard_map/ckn,nj->ckj/dot_general | solution.py:46
  53.0 74.5 %all-gather.6.cloned.1.call-done = bf16[4096,1024]{1,0:T(8,128)(2,1)} async-done(((bf16[512,1024]{1,0:T(8,128)(2,1)}), bf16[4096,1024]{1,0:T(8,128)(2,1)}) %all-gather.6.cloned.1.call-update) | async-done | bytes 8388624 | tf_op jit(solution)/shard_map/all_gather | solution.py:80
  127.5 79.9 %all-gather.4.cloned.1.call-done = bf16[3,4096,512]{1,2,0:T(8,128)(2,1)} async-done(((bf16[3,256,512]{1,2,0:T(8,128)(2,1)}), bf16[3,4096,512]{1,2,0:T(8,128)(2,1)}) %all-gather.4.cloned.1.call-update) | async-done | bytes 12582928 | tf_op jit(solution)/shard_map/all_gather | solution.py:82
  207.3 16.7 %fusion = f32[3,512,1024]{2,1,0:T(8,128)S(1)} fusion(bf16[3,4096,512]{1,2,0:T(8,128)(2,1)} %all-gather.4.cloned.1.call-done, bf16[4096,1024]{1,0:T(8,128)(2,1)} %all-gather.6.cloned.1.call-done), kind=kOutput, calls=%fused_computation | convolution fusion | flops 12884901888 | bytes 27262976 | tf_op jit(solution)/shard_map/sic,it->sct/dot_general | solution.py:85
  230.0 8.5 %fusion.34 = f32[32,256,128]{2,1,0:T(8,128)} fusion(f32[32,256,128]{2,1,0:T(8,128)} %fusion.6, f32[256,32,128]{2,0,1:T(8,128)} %copy-done, f32[256,32,128]{2,0,1:T(8,128)} %copy-done.2, f32[256,128]{1,0:T(8,128)S(1)} %get-tuple-element.12, f32[256,128]{1,0:T(8,128)S(1)} %get-tuple-element.13), kind=kOutput, calls=%fused_computation.39 | convolution fusion | flops 1616084992 | bytes 17039360 | tf_op jit(solution)/shard_map/ckn,nj->ckj/dot_general | solution.py:46
  239.1 9.3 %fusion.3 = f32[3,512,1024]{2,1,0:T(8,128)S(1)} fusion(f32[3,512,1023]{2,1,0:T(8,128)} %bitcast.120, f32[3,512,1]{2,1,0:T(8,128)S(1)} %copy.27, f32[3,512,1022]{2,1,0:T(8,128)} %bitcast.121, f32[3,512,2]{2,1,0:T(8,128)S(1)} %copy.28, f32[3,512,1024]{2,1,0:T(8,128)} %copy-done.4, f32[3,512]{1,0:T(4,128)S(1)} %get-tuple-element.10, ...), kind=kLoop, calls=%fused_computation.5 | loop fusion | flops 11010048 | bytes 25184256 | tf_op jit(solution)/shard_map/add | solution.py:94
  252.3 4.5 all-to-all-start
  256.9 6.8 %fusion.4 = f32[32,256,128]{2,1,0:T(8,128)S(1)} fusion(f32[256,32,128]{2,0,1:T(8,128)} %copy-done, f32[256,32,128]{2,0,1:T(8,128)} %copy-done.2, f32[256,128]{1,0:T(8,128)S(1)} %get-tuple-element.12, f32[256,128]{1,0:T(8,128)S(1)} %get-tuple-element.13), kind=kOutput, calls=%fused_computation.7 | convolution fusion | flops 1615036416 | bytes 12845056 | tf_op jit(solution)/shard_map/ckn,nj->ckj/dot_general | solution.py:49
  263.7 5.7 %fusion.37 = f32[32,256,128]{2,1,0:T(8,128)} fusion(f32[32,256,128]{2,1,0:T(8,128)S(1)} %fusion.4, f32[256,32,128]{2,0,1:T(8,128)S(1)} %copy-done.1, f32[256,32,128]{2,0,1:T(8,128)S(1)} %copy-done.3, f32[256,128]{1,0:T(8,128)S(1)} %get-tuple-element.12, f32[256,128]{1,0:T(8,128)S(1)} %get-tuple-element.13), kind=kOutput, calls=%fused_computation.40 | convolution fusion | flops 1616084992 | bytes 17039360 | tf_op jit(solution)/shard_map/ckn,nj->ckj/dot_general | solution.py:49
  278.8 4.3 fusion.14
  283.2 5.5 %fusion.12 = f32[32,256,128]{2,1,0:T(8,128)S(1)} fusion(f32[256,32,128]{2,0,1:T(8,128)S(1)} %fusion.66, f32[256,32,128]{2,0,1:T(8,128)S(1)} %fusion.62, f32[256,128]{1,0:T(8,128)} %copy-done.6, f32[256,128]{1,0:T(8,128)} %copy-done.9), kind=kOutput, calls=%fused_computation.15 | convolution fusion | flops 1615036416 | bytes 12845056 | tf_op jit(solution)/shard_map/ckn,nj->ckj/dot_general | solution.py:49
  288.7 5.7 %fusion.28 = f32[32,256,128]{2,1,0:T(8,128)} fusion(f32[32,256,128]{2,1,0:T(8,128)S(1)} %fusion.14, f32[256,32,128]{2,0,1:T(8,128)S(1)} %fusion.66, f32[256,32,128]{2,0,1:T(8,128)S(1)} %fusion.62, f32[256,128]{1,0:T(8,128)S(1)} %copy-done.7, f32[256,128]{1,0:T(8,128)S(1)} %copy-done.10), kind=kOutput, calls=%fused_computation.37 | convolution fusion | flops 1616084992 | bytes 17039360 | tf_op jit(solution)/shard_map/ckn,nj->ckj/dot_general | solution.py:46
  294.4 8.4 %multiply_add_fusion = (f32[32,256,128]{2,1,0:T(8,128)S(1)}, f32[32,256,128]{2,1,0:T(8,128)S(1)}) fusion(f32[32,256,128]{2,1,0:T(8,128)} %fusion.34, f32[32,256,128]{2,1,0:T(8,128)} %fusion.28, f32[32,256,128]{2,1,0:T(8,128)} %fusion.37, f32[32,256,128]{2,1,0:T(8,128)S(1)} %fusion.12, f32[256,128]{1,0:T(8,128)} %copy-done.6, ...), kind=kOutput, calls=%fused_computation.31 | convolution fusion | flops 1622376448 | bytes 33816576 | tf_op jit(solution)/shard_map/ckn,nj->ckj/dot_general | solution.py:49
  302.8 3.7 fusion.86
  306.5 3.7 fusion.84
  310.1 3.7 convolution_subtract_fusion
  313.8 3.9 convolution_add_fusion
  321.0 3.4 fusion.50
  325.5 19.1 %all_to_all.39 = bf16[32,16,1024]{2,0,1:T(8,128)(2,1)S(1)} all-to-all(bf16[32,16,1024]{2,0,1:T(8,128)(2,1)S(1)} %copy.35), channel_id=1, replica_groups=mesh['ctx'=16,'tp'=8] {'ctx'}, dimensions={1} | all-to-all | bytes 2097152 | tf_op jit(solution)/shard_map/all_to_all | solution.py:107
  344.6 3.4 fusion.41
  348.0 9.0 %convert_bitcast_fusion = bf16[4096,1024]{0,1:T(8,128)(2,1)} fusion(bf16[512,1024]{1,0:T(8,128)(2,1)S(1)} %fusion.41, bf16[512,4096]{1,0:T(8,128)(2,1)} %all-gather.8.cloned.1.call-done), kind=kOutput, calls=%fused_computation.2 | convolution fusion | flops 4299161600 | bytes 13631488 | tf_op jit(solution)/shard_map/cd,ct->dt/dot_general | solution.py:114
  357.0 113.9 %reduce-scatter.2.cloned.1.call-done = bf16[512,1024]{0,1:T(8,128)(2,1)} async-done(((bf16[4096,1024]{0,1:T(8,128)(2,1)}), bf16[512,1024]{0,1:T(8,128)(2,1)}) %reduce-scatter.2.cloned.1.call-update) | async-done | bytes 1048592 | tf_op jit(solution)/shard_map/reduce_scatter | solution.py:113
  (66 shorter events, 39.8 us)
Async XLA Ops:
  6.5 3.1 copy-start.12
  6.5 120.9 %all-gather.6.cloned.1.call-start = ((), (), s32[]{:S(2)}) async-start(), calls=%async_computation.5 | async-start | bytes 9437184 | tf_op jit(solution)/shard_map/all_gather | solution.py:80
  7.3 12.1 %copy-start.13 = (f32[3,512,3]{1,2,0:T(4,128)S(1)}, f32[3,512,3]{1,2,0:T(4,128)}, u32[]{:S(2)}) copy-start(f32[3,512,3]{1,2,0:T(4,128)} %param.8) | copy-start | bytes 55300
  7.3 200.1 %all-gather.4.cloned.1.call-start = ((), (), s32[]{:S(2)}) async-start(), calls=%async_computation.4 | async-start | bytes 13369344 | tf_op jit(solution)/shard_map/all_gather | solution.py:82
  10.8 28.8 %all-to-all-start.1 = ((bf16[16,32,1024]{2,1,0:T(8,128)(2,1)}), bf16[16,32,1024]{2,1,0:T(8,128)(2,1)S(1)}, u32[]{:S(2)}, u32[]{:S(2)}) async-start(bf16[16,32,1024]{2,1,0:T(8,128)(2,1)} %bitcast.11), calls=%async_computation.1 | async-start | bytes 2097152 | tf_op jit(solution)/shard_map/all_to_all | solution.py:77
  18.6 329.4 %all-gather.8.cloned.1.call-start = ((), (), s32[]{:S(2)}) async-start(), calls=%async_computation.6 | async-start | bytes 4456448 | tf_op jit(solution)/shard_map/all_gather | solution.py:112
  20.0 258.9 %copy-start.6 = (f32[256,128]{1,0:T(8,128)}, f32[256,128]{1,0:T(8,128)S(1)}, u32[]{:S(2)}) copy-start(f32[256,128]{1,0:T(8,128)S(1)} %get-tuple-element.12) | copy-start | bytes 393220
  20.0 258.9 %copy-start.9 = (f32[256,128]{1,0:T(8,128)}, f32[256,128]{1,0:T(8,128)S(1)}, u32[]{:S(2)}) copy-start(f32[256,128]{1,0:T(8,128)S(1)} %get-tuple-element.13) | copy-start | bytes 393220
  43.1 2.4 copy-start
  45.4 2.0 copy-start.2
  224.1 2.6 copy-start.4
  227.2 11.3 %collective-permute-start = (f32[3,512,2]{1,2,0:T(2,128)S(1)}, f32[3,512,2]{1,2,0:T(2,128)S(1)}, u32[]{:S(2)}, u32[]{:S(2)}) collective-permute-start(f32[3,512,2]{1,2,0:T(2,128)S(1)} %copy.26), channel_id=1, source_target_pairs={{0,8},{8,16},{16,24},{24,32},{32,40},{40,48},{48,56},{56,64},{64,7... | collective-permute-start | bytes 36872 | tf_op jit(solution)/shard_map/ppermute | solution.py:13
  248.4 2.6 copy-start.5
  252.3 20.3 %all-to-all-start = ((bf16[16,32,1024]{2,1,0:T(8,128)(2,1)}), bf16[16,32,1024]{2,1,0:T(8,128)(2,1)S(1)}, u32[]{:S(2)}, u32[]{:S(2)}) async-start(bf16[16,32,1024]{2,1,0:T(8,128)(2,1)} %bitcast.3), calls=%async_computation | async-start | bytes 2097152 | tf_op jit(solution)/shard_map/all_to_all | solution.py:99
  256.9 214.1 %reduce-scatter.2.cloned.1.call-start = ((), (), s32[]{:S(2)}) async-start(), calls=%async_computation.7 | async-start | bytes 9437184 | tf_op jit(solution)/shard_map/reduce_scatter | solution.py:113
  256.9 6.8 %copy-start.1 = (f32[256,32,128]{2,0,1:T(8,128)S(1)}, f32[256,32,128]{2,0,1:T(8,128)}, u32[]{:S(2)}) copy-start(f32[256,32,128]{2,0,1:T(8,128)} %copy-done) | copy-start | bytes 12582916
  256.9 6.8 %copy-start.3 = (f32[256,32,128]{2,0,1:T(8,128)S(1)}, f32[256,32,128]{2,0,1:T(8,128)}, u32[]{:S(2)}) copy-start(f32[256,32,128]{2,0,1:T(8,128)} %copy-done.2) | copy-start | bytes 12582916
  283.2 5.5 %copy-start.7 = (f32[256,128]{1,0:T(8,128)S(1)}, f32[256,128]{1,0:T(8,128)}, u32[]{:S(2)}) copy-start(f32[256,128]{1,0:T(8,128)} %copy-done.6) | copy-start | bytes 393220
  283.2 5.5 %copy-start.10 = (f32[256,128]{1,0:T(8,128)S(1)}, f32[256,128]{1,0:T(8,128)}, u32[]{:S(2)}) copy-start(f32[256,128]{1,0:T(8,128)} %copy-done.9) | copy-start | bytes 393220
  313.8 3.9 copy-start.8
  313.8 3.9 copy-start.11
  324.4 20.2 %copy-start.14 = (f32[512]{0:T(512)S(1)}, f32[512]{0:T(512)}, u32[]{:S(2)}) copy-start(f32[512]{0:T(512)} %param.10) | copy-start | bytes 6148
Sparse Core Ops, SparseCore 0:
  9.7 117.7 all-gather.5
  129.1 78.2 all-gather.3
  209.0 45.4 all-gather.7
  357.2 113.7 reduce-scatter.1
where the time goes:
time: 489 us; the launch traced here: 480 us
  waiting for transfers between devices  293 us (60%)
  matrix products  107 us (22%)
  blocking collectives  19.1 us (4%)
  local copies, waits for them, and re-layouts  16.7 us (3%)
  other arithmetic  15.6 us (3%)
  starting transfers between devices  15.3 us (3%)
  between operations  14 us (3%)
    reduce_scatter x1, waiting for transfers between devices, per_device(): lax.psum_scatter(jnp.einsum('cd,ct->dt', whole_out, hidden, preferred_ele...  114 us
    all_gather x1, waiting for transfers between devices, per_device(): shard_rows = lax.all_gather(in_weight, 'ctx', axis=1, tiled=True)  79.9 us
    all_gather x1, waiting for transfers between devices, per_device(): features_all = lax.all_gather(tokens, 'tp', axis=0, tiled=True)  74.5 us
    all_to_all x1, waiting for transfers between devices, per_device(): lax.all_to_all(long_filter.astype(jnp.bfloat16), 'ctx', split_axis=0, con...  19.7 us
    all_to_all x1, blocking collectives, per_device(): lax.all_to_all(long_rows, 'ctx', split_axis=1, concat_axis=0, tiled=True)  19.1 us
    dot_general x1, matrix products, per_device(): jnp.einsum('sic,it->sct', shard_rows, source, preferred_element_type=jnp....  16.7 us
    dot_general x2, matrix products, spectrum(): jnp.einsum('ckn,nj->ckj', twist_re, sin_inner, precision=HIGHEST)  14.1 us
    dot_general x2, matrix products, spectrum(): jnp.einsum('ckn,nj->ckj', twist_re, cos_inner, precision=HIGHEST)  14.1 us
  transfers between devices with their start and end apart: 7, of which 5 were waited for; matrix products, arithmetic and copies ran while one was open for 25% of the time, Pallas kernels for 0%

commit v1 on v0

--- a/solution.py
+++ b/solution.py
@@ -79,7 +79,8 @@
     ).astype(long_filter.dtype)
     features_all = lax.all_gather(tokens, "tp", axis=0, tiled=True)
     sources = (features_all,)
-    shard_rows = lax.all_gather(in_weight, "ctx", axis=1, tiled=True)
+    repeated = jnp.stack([in_weight] * lax.axis_size("ctx"))
+    shard_rows = jnp.concatenate(lax.all_to_all(repeated, "ctx", 0, 0), axis=1)
     results = tuple(
         (
             jnp.einsum("sic,it->sct", shard_rows, source, preferred_element_type=jnp.float32)

time: 489 us -> 561 us (1.15)
  waiting for transfers between devices: 293 us -> 338 us
  local copies, waits for them, and re-layouts: 16.7 us -> 31.3 us
  starting transfers between devices: 15.3 us -> 25.2 us
    all_to_all x0 -> x1, waiting for transfers between devices: none -> 199 us  [per_device(): shard_rows = jnp.concatenate(lax.all_to_all(repeated, 'ctx', 0, 0), axis=1)]
    all_gather x1 -> x0, waiting for transfers between devices: 79.9 us -> none  [per_device(): shard_rows = lax.all_gather(in_weight, 'ctx', axis=1, tiled=True)]
    all_gather x1, waiting for transfers between devices: 74.5 us -> 0.01 us  [per_device(): features_all = lax.all_gather(tokens, 'tp', axis=0, tiled=True)]
    reshape x0 -> x1, local copies, waits for them, and re-layouts: none -> 10.8 us  [per_device(): shard_rows = jnp.concatenate(lax.all_to_all(repeated, 'ctx', 0, 0), axis=1)]
    all_to_all x0 -> x1, starting transfers between devices: none -> 6.53 us  [per_device(): shard_rows = jnp.concatenate(lax.all_to_all(repeated, 'ctx', 0, 0), axis=1)]
    another operation x0 -> x1, local copies, waits for them, and re-layouts: none -> 6 us  [per_device(): repeated = jnp.stack([in_weight] * lax.axis_size('ctx'))]
  transfers between devices with their start and end apart: 7 -> 7, of which waited for: 5 -> 4; matrix products, arithmetic and copies ran while one was open for 25% -> 25% of each run, Pallas kernels for 0% -> 0%
where the time goes in v1:
time: 561 us; the launch traced here: 551 us
  waiting for transfers between devices  338 us (60%)
  matrix products  107 us (19%)
  local copies, waits for them, and re-layouts  31.3 us (6%)
  starting transfers between devices  25.2 us (4%)
  blocking collectives  19.1 us (3%)
  other arithmetic  16.9 us (3%)
  between operations  14 us (2%)
    all_to_all x1, waiting for transfers between devices, per_device(): shard_rows = jnp.concatenate(lax.all_to_all(repeated, 'ctx', 0, 0), axis=1)  199 us
    reduce_scatter x1, waiting for transfers between devices, per_device(): lax.psum_scatter(jnp.einsum('cd,ct->dt', whole_out, hidden, preferred_ele...  114 us
    all_to_all x1, waiting for transfers between devices, per_device(): lax.all_to_all(long_filter.astype(jnp.bfloat16), 'ctx', split_axis=0, con...  19.9 us
    all_to_all x1, blocking collectives, per_device(): lax.all_to_all(long_rows, 'ctx', split_axis=1, concat_axis=0, tiled=True)  19.1 us
    dot_general x1, matrix products, per_device(): jnp.einsum('sic,it->sct', shard_rows, source, preferred_element_type=jnp....  16.7 us
    dot_general x2, matrix products, spectrum(): jnp.einsum('ckn,nj->ckj', twist_re, sin_inner, precision=HIGHEST)  14.2 us
    dot_general x2, matrix products, spectrum(): jnp.einsum('ckn,nj->ckj', twist_re, cos_inner, precision=HIGHEST)  14.2 us
    dot_general x2, matrix products, spectrum(): jnp.einsum('ckn,nj->ckj', twist_im, cos_inner, precision=HIGHEST)  12.2 us
  transfers between devices with their start and end apart: 7, of which 4 were waited for; matrix products, arithmetic and copies ran while one was open for 25% of the time, Pallas kernels for 0%

profile of v1, /device:TPU:1, one launch (start us, length us, event | category | flops | bytes accessed | tf_op | source)
XLA Modules:
  0.0 551.3 jit_solution(4148582532454923882)
XLA Ops:
  10.0 7.8 %all-to-all-start.2 = ((bf16[16,32,1024]{2,1,0:T(8,128)(2,1)}), bf16[16,32,1024]{2,1,0:T(8,128)(2,1)S(1)}, u32[]{:S(2)}, u32[]{:S(2)}) async-start(bf16[16,32,1024]{2,1,0:T(8,128)(2,1)} %bitcast.12), calls=%async_computation.2 | async-start | bytes 2097152 | tf_op jit(solution)/shard_map/all_to_all | solution.py:77
  18.1 19.9 %all-to-all-done.2 = bf16[16,32,1024]{2,1,0:T(8,128)(2,1)S(1)} async-done(((bf16[16,32,1024]{2,1,0:T(8,128)(2,1)}), bf16[16,32,1024]{2,1,0:T(8,128)(2,1)S(1)}, u32[]{:S(2)}, u32[]{:S(2)}) %all-to-all-start.2) | async-done | bytes 1048608 | tf_op jit(solution)/shard_map/all_to_all | solution.py:77
  38.0 6.0 %stack.2 = bf16[16,3,256,512]{2,3,1,0:T(8,128)(2,1)} broadcast(bf16[3,256,512]{1,2,0:T(8,128)(2,1)S(1)} %copy.25), dimensions={1,2,3} | broadcast | bytes 13369344 | tf_op jit(solution)/shard_map/stack | solution.py:82
  44.0 6.5 %all-to-all-start = ((bf16[16,3,256,512]{2,3,1,0:T(8,128)(2,1)}), bf16[16,3,256,512]{2,3,1,0:T(8,128)(2,1)}, u32[]{:S(2)}, u32[]{:S(2)}) async-start(bf16[16,3,256,512]{2,3,1,0:T(8,128)(2,1)} %stack.2), calls=%async_computation | async-start | bytes 25165824 | tf_op jit(solution)/shard_map/all_to_all | solution.py:83
  59.7 5.7 %fusion.6 = f32[32,256,128]{2,1,0:T(8,128)} fusion(f32[256,32,128]{2,0,1:T(8,128)S(1)} %fusion.64, f32[256,32,128]{2,0,1:T(8,128)S(1)} %fusion.60, f32[256,128]{1,0:T(8,128)S(1)} %get-tuple-element.12, f32[256,128]{1,0:T(8,128)S(1)} %get-tuple-element.13), kind=kOutput, calls=%fused_computation.9 | convolution fusion | flops 1615036416 | bytes 12845056 | tf_op jit(solution)/shard_map/ckn,nj->ckj/dot_general | solution.py:46
  65.3 198.9 %all-to-all-done = bf16[16,3,256,512]{2,3,1,0:T(8,128)(2,1)} async-done(((bf16[16,3,256,512]{2,3,1,0:T(8,128)(2,1)}), bf16[16,3,256,512]{2,3,1,0:T(8,128)(2,1)}, u32[]{:S(2)}, u32[]{:S(2)}) %all-to-all-start) | async-done | bytes 12582944 | tf_op jit(solution)/shard_map/all_to_all | solution.py:83
  264.2 10.8 %copy.49 = bf16[16,3,64,8,256]{4,3,0,2,1:T(8,128)(2,1)} copy(bf16[16,3,64,8,256]{4,3,2,1,0:T(8,128)(2,1)} %bitcast.29) | data formatting | bytes 25165824 | tf_op jit(solution)/shard_map/reshape | solution.py:83
  275.0 16.7 %fusion = f32[3,512,1024]{2,1,0:T(8,128)S(1)} fusion(bf16[3,4096,512]{1,2,0:T(8,128)(2,1)} %bitcast.125, bf16[4096,1024]{1,0:T(8,128)(2,1)} %all-gather.3.cloned.1.call-done), kind=kOutput, calls=%fused_computation | convolution fusion | flops 12884901888 | bytes 27262976 | tf_op jit(solution)/shard_map/sic,it->sct/dot_general | solution.py:86
  297.0 8.5 %fusion.34 = f32[32,256,128]{2,1,0:T(8,128)} fusion(f32[32,256,128]{2,1,0:T(8,128)} %fusion.6, f32[256,32,128]{2,0,1:T(8,128)} %copy-done, f32[256,32,128]{2,0,1:T(8,128)} %copy-done.2, f32[256,128]{1,0:T(8,128)S(1)} %get-tuple-element.12, f32[256,128]{1,0:T(8,128)S(1)} %get-tuple-element.13), kind=kOutput, calls=%fused_computation.39 | convolution fusion | flops 1616084992 | bytes 17039360 | tf_op jit(solution)/shard_map/ckn,nj->ckj/dot_general | solution.py:46
  306.1 8.9 %fusion.3 = f32[3,512,1024]{2,1,0:T(8,128)S(1)} fusion(f32[3,512,1023]{2,1,0:T(8,128)} %bitcast.123, f32[3,512,1]{2,1,0:T(8,128)S(1)} %copy.28, f32[3,512,1022]{2,1,0:T(8,128)} %bitcast.124, f32[3,512,2]{2,1,0:T(8,128)S(1)} %copy.29, f32[3,512,1024]{2,1,0:T(8,128)} %copy-done.4, f32[3,512]{1,0:T(4,128)S(1)} %get-tuple-element.10, ...), kind=kLoop, calls=%fused_computation.5 | loop fusion | flops 11010048 | bytes 25184256 | tf_op jit(solution)/shard_map/add | solution.py:95
  319.0 8.6 %all-to-all-start.1 = ((bf16[16,32,1024]{2,1,0:T(8,128)(2,1)}), bf16[16,32,1024]{2,1,0:T(8,128)(2,1)S(1)}, u32[]{:S(2)}, u32[]{:S(2)}) async-start(bf16[16,32,1024]{2,1,0:T(8,128)(2,1)} %bitcast.4), calls=%async_computation.1 | async-start | bytes 2097152 | tf_op jit(solution)/shard_map/all_to_all | solution.py:100
  327.7 6.8 %fusion.4 = f32[32,256,128]{2,1,0:T(8,128)S(1)} fusion(f32[256,32,128]{2,0,1:T(8,128)} %copy-done, f32[256,32,128]{2,0,1:T(8,128)} %copy-done.2, f32[256,128]{1,0:T(8,128)S(1)} %get-tuple-element.12, f32[256,128]{1,0:T(8,128)S(1)} %get-tuple-element.13), kind=kOutput, calls=%fused_computation.7 | convolution fusion | flops 1615036416 | bytes 12845056 | tf_op jit(solution)/shard_map/ckn,nj->ckj/dot_general | solution.py:49
  334.5 5.8 %fusion.37 = f32[32,256,128]{2,1,0:T(8,128)} fusion(f32[32,256,128]{2,1,0:T(8,128)S(1)} %fusion.4, f32[256,32,128]{2,0,1:T(8,128)S(1)} %copy-done.1, f32[256,32,128]{2,0,1:T(8,128)S(1)} %copy-done.3, f32[256,128]{1,0:T(8,128)S(1)} %get-tuple-element.12, f32[256,128]{1,0:T(8,128)S(1)} %get-tuple-element.13), kind=kOutput, calls=%fused_computation.40 | convolution fusion | flops 1616084992 | bytes 17039360 | tf_op jit(solution)/shard_map/ckn,nj->ckj/dot_general | solution.py:49
  349.6 4.3 fusion.14
  353.9 5.5 fusion.12
  359.4 5.7 %fusion.28 = f32[32,256,128]{2,1,0:T(8,128)} fusion(f32[32,256,128]{2,1,0:T(8,128)S(1)} %fusion.14, f32[256,32,128]{2,0,1:T(8,128)S(1)} %fusion.66, f32[256,32,128]{2,0,1:T(8,128)S(1)} %fusion.62, f32[256,128]{1,0:T(8,128)S(1)} %copy-done.7, f32[256,128]{1,0:T(8,128)S(1)} %copy-done.10), kind=kOutput, calls=%fused_computation.37 | convolution fusion | flops 1616084992 | bytes 17039360 | tf_op jit(solution)/shard_map/ckn,nj->ckj/dot_general | solution.py:46
  365.2 8.4 %multiply_add_fusion = (f32[32,256,128]{2,1,0:T(8,128)S(1)}, f32[32,256,128]{2,1,0:T(8,128)S(1)}) fusion(f32[32,256,128]{2,1,0:T(8,128)} %fusion.34, f32[32,256,128]{2,1,0:T(8,128)} %fusion.28, f32[32,256,128]{2,1,0:T(8,128)} %fusion.37, f32[32,256,128]{2,1,0:T(8,128)S(1)} %fusion.12, f32[256,128]{1,0:T(8,128)} %copy-done.6, ...), kind=kOutput, calls=%fused_computation.31 | convolution fusion | flops 1622376448 | bytes 33816576 | tf_op jit(solution)/shard_map/ckn,nj->ckj/dot_general | solution.py:49
  373.6 3.7 fusion.86
  377.2 3.7 fusion.84
  380.9 3.7 convolution_subtract_fusion
  384.6 3.9 convolution_add_fusion
  396.3 19.1 %all_to_all.44 = bf16[32,16,1024]{2,0,1:T(8,128)(2,1)S(1)} all-to-all(bf16[32,16,1024]{2,0,1:T(8,128)(2,1)S(1)} %copy.36), channel_id=1, replica_groups=mesh['ctx'=16,'tp'=8] {'ctx'}, dimensions={1} | all-to-all | bytes 2097152 | tf_op jit(solution)/shard_map/all_to_all | solution.py:108
  418.8 9.0 %convert_bitcast_fusion = bf16[4096,1024]{0,1:T(8,128)(2,1)} fusion(bf16[512,1024]{1,0:T(8,128)(2,1)S(1)} %fusion.41, bf16[512,4096]{1,0:T(8,128)(2,1)} %all-gather.5.cloned.1.call-done), kind=kOutput, calls=%fused_computation.2 | convolution fusion | flops 4299161600 | bytes 13631488 | tf_op jit(solution)/shard_map/cd,ct->dt/dot_general | solution.py:115
  427.8 114.3 %reduce-scatter.2.cloned.1.call-done = bf16[512,1024]{0,1:T(8,128)(2,1)} async-done(((bf16[4096,1024]{0,1:T(8,128)(2,1)}), bf16[512,1024]{0,1:T(8,128)(2,1)}) %reduce-scatter.2.cloned.1.call-update) | async-done | bytes 1048592 | tf_op jit(solution)/shard_map/reduce_scatter | solution.py:114
  (67 shorter events, 45.2 us)
Async XLA Ops:
  6.5 11.3 %copy-start.12 = (bf16[3,256,512]{2,1,0:T(8,128)(2,1)S(1)}, bf16[3,256,512]{2,1,0:T(8,128)(2,1)}, u32[]{:S(2)}) copy-start(bf16[3,256,512]{2,1,0:T(8,128)(2,1)} %param.7) | copy-start | bytes 2359300
  6.5 268.5 %all-gather.3.cloned.1.call-start = ((), (), s32[]{:S(2)}) async-start(), calls=%async_computation.5 | async-start | bytes 9437184 | tf_op jit(solution)/shard_map/all_gather | solution.py:80
  10.0 28.0 %all-to-all-start.2 = ((bf16[16,32,1024]{2,1,0:T(8,128)(2,1)}), bf16[16,32,1024]{2,1,0:T(8,128)(2,1)S(1)}, u32[]{:S(2)}, u32[]{:S(2)}) async-start(bf16[16,32,1024]{2,1,0:T(8,128)(2,1)} %bitcast.12), calls=%async_computation.2 | async-start | bytes 2097152 | tf_op jit(solution)/shard_map/all_to_all | solution.py:77
  44.0 7.3 %copy-start.13 = (f32[3,512,3]{1,2,0:T(4,128)S(1)}, f32[3,512,3]{1,2,0:T(4,128)}, u32[]{:S(2)}) copy-start(f32[3,512,3]{1,2,0:T(4,128)} %param.8) | copy-start | bytes 55300
  44.0 220.2 %all-to-all-start = ((bf16[16,3,256,512]{2,3,1,0:T(8,128)(2,1)}), bf16[16,3,256,512]{2,3,1,0:T(8,128)(2,1)}, u32[]{:S(2)}, u32[]{:S(2)}) async-start(bf16[16,3,256,512]{2,3,1,0:T(8,128)(2,1)} %stack.2), calls=%async_computation | async-start | bytes 25165824 | tf_op jit(solution)/shard_map/all_to_all | solution.py:83
  50.6 368.2 %all-gather.5.cloned.1.call-start = ((), (), s32[]{:S(2)}) async-start(), calls=%async_computation.6 | async-start | bytes 4456448 | tf_op jit(solution)/shard_map/all_gather | solution.py:113
  51.9 297.7 %copy-start.6 = (f32[256,128]{1,0:T(8,128)}, f32[256,128]{1,0:T(8,128)S(1)}, u32[]{:S(2)}) copy-start(f32[256,128]{1,0:T(8,128)S(1)} %get-tuple-element.12) | copy-start | bytes 393220
  51.9 297.7 %copy-start.9 = (f32[256,128]{1,0:T(8,128)}, f32[256,128]{1,0:T(8,128)S(1)}, u32[]{:S(2)}) copy-start(f32[256,128]{1,0:T(8,128)S(1)} %get-tuple-element.13) | copy-start | bytes 393220
  55.3 2.4 copy-start
  57.7 2.0 copy-start.2
  291.7 2.6 copy-start.4
  294.9 10.6 %collective-permute-start = (f32[3,512,2]{1,2,0:T(2,128)S(1)}, f32[3,512,2]{1,2,0:T(2,128)S(1)}, u32[]{:S(2)}, u32[]{:S(2)}) collective-permute-start(f32[3,512,2]{1,2,0:T(2,128)S(1)} %copy.27), channel_id=1, source_target_pairs={{0,8},{8,16},{16,24},{24,32},{32,40},{40,48},{48,56},{56,64},{64,7... | collective-permute-start | bytes 36872 | tf_op jit(solution)/shard_map/ppermute | solution.py:13
  315.0 2.6 copy-start.5
  319.0 24.5 %all-to-all-start.1 = ((bf16[16,32,1024]{2,1,0:T(8,128)(2,1)}), bf16[16,32,1024]{2,1,0:T(8,128)(2,1)S(1)}, u32[]{:S(2)}, u32[]{:S(2)}) async-start(bf16[16,32,1024]{2,1,0:T(8,128)(2,1)} %bitcast.4), calls=%async_computation.1 | async-start | bytes 2097152 | tf_op jit(solution)/shard_map/all_to_all | solution.py:100
  327.6 214.4 %reduce-scatter.2.cloned.1.call-start = ((), (), s32[]{:S(2)}) async-start(), calls=%async_computation.7 | async-start | bytes 9437184 | tf_op jit(solution)/shard_map/reduce_scatter | solution.py:114
  327.7 6.8 %copy-start.1 = (f32[256,32,128]{2,0,1:T(8,128)S(1)}, f32[256,32,128]{2,0,1:T(8,128)}, u32[]{:S(2)}) copy-start(f32[256,32,128]{2,0,1:T(8,128)} %copy-done) | copy-start | bytes 12582916
  327.7 6.8 %copy-start.3 = (f32[256,32,128]{2,0,1:T(8,128)S(1)}, f32[256,32,128]{2,0,1:T(8,128)}, u32[]{:S(2)}) copy-start(f32[256,32,128]{2,0,1:T(8,128)} %copy-done.2) | copy-start | bytes 12582916
  353.9 5.5 %copy-start.7 = (f32[256,128]{1,0:T(8,128)S(1)}, f32[256,128]{1,0:T(8,128)}, u32[]{:S(2)}) copy-start(f32[256,128]{1,0:T(8,128)} %copy-done.6) | copy-start | bytes 393220
  353.9 5.5 %copy-start.10 = (f32[256,128]{1,0:T(8,128)S(1)}, f32[256,128]{1,0:T(8,128)}, u32[]{:S(2)}) copy-start(f32[256,128]{1,0:T(8,128)} %copy-done.9) | copy-start | bytes 393220
  384.6 3.9 copy-start.8
  384.6 3.9 copy-start.11
  395.2 20.2 %copy-start.14 = (f32[512]{0:T(512)S(1)}, f32[512]{0:T(512)}, u32[]{:S(2)}) copy-start(f32[512]{0:T(512)} %param.10) | copy-start | bytes 6148
Sparse Core Ops, SparseCore 0:
  9.7 162.4 all-gather.2
  173.8 88.1 all-gather.4
  427.9 114.0 reduce-scatter.1
